TPU v7x, 32 devices: a whole 2x2x4 slice. The times are simulated.
32 devices in a mesh: seq: 4 (over z), dp: 8 (over y, x, core).
Axes of the slice: x: 2, y: 2, z: 4, core: 2. Of those that a mesh axis runs over, the one named last changes fastest.
Arguments:
- tokens: bfloat16 [8, 1024, 768], P('dp', 'seq'), may hold values from -6 to 6
- qkv_weight: bfloat16 [768, 2304], P('dp'), may hold values from -0.21875 to 0.21875
- proj_weight: bfloat16 [768, 768], P('dp'), may hold values from -0.875 to 0.875
- hidden_weight: bfloat16 [768, 3072], P('dp'), may hold values from -0.21875 to 0.21875
- output_weight: bfloat16 [3072, 768], P('dp'), may hold values from -0.109375 to 0.109375
- first_gain: bfloat16 [768], P('dp'), may hold values from 0.25 to 1.75
- first_bias: bfloat16 [768], P('dp'), may hold values from -2.5 to 2.5
- second_gain: bfloat16 [768], P('dp'), may hold values from 0.25 to 1.75
- second_bias: bfloat16 [768], P('dp'), may hold values from -2.5 to 2.5
- cotangent: bfloat16 [8, 1024, 768], P('dp', 'seq'), may hold values from -6 to 6
Outputs:
- block_out: bfloat16 [8, 1024, 768], P('dp', 'seq')
- tokens_gradient: bfloat16 [8, 1024, 768], P('dp', 'seq')
- qkv_gradient: float32 [768, 2304], P('dp')
- proj_gradient: float32 [768, 768], P('dp')
- hidden_gradient: float32 [768, 3072], P('dp')
- output_gradient: float32 [3072, 768], P('dp')
- first_gain_gradient: float32 [768], P('dp')
- first_bias_gradient: float32 [768], P('dp')
- second_gain_gradient: float32 [768], P('dp')
- second_bias_gradient: float32 [768], P('dp')
All inputs are finite; a program needn't handle non-finite values.
Results may differ from a plain program's by a relative error of at most 0.012.
Values may be sent and summed in bfloat16 or wider, within the bound.
A program may use at most 256 MiB of HBM per device.

v0:
```python
import jax
import jax.numpy as jnp
from jax import lax
from jax.sharding import PartitionSpec as P

HEAD_DIM = 64
LOW = jnp.bfloat16
F32 = jnp.float32


def layer_norm(values, gain, bias):
    average = jnp.mean(values, -1, keepdims=True)
    centred = values - average
    variance = jnp.mean(centred * centred, -1, keepdims=True)
    return centred * lax.rsqrt(variance + 1e-05) * gain + bias


def gelu_tanh(values):
    return jax.nn.gelu(values, approximate=True)


def matmul(left, right):
    return jnp.dot(left, right, preferred_element_type=F32)


def matmul_left_t(left, right):
    return lax.dot_general(left, right, (((0,), (0,)), ((), ())), preferred_element_type=F32)


def matmul_right_t(left, right):
    return lax.dot_general(left, right, (((1,), (1,)), ((), ())), preferred_element_type=F32)


def gather_seq(value):
    return lax.all_gather(value, "seq", axis=0, tiled=True)


def scatter_seq(value):
    return lax.psum_scatter(value.astype(LOW), "seq", scatter_dimension=0, tiled=True).astype(F32)


def attention_forward(queries, keys, values):
    length, local_width = queries.shape
    heads_here = local_width // HEAD_DIM
    block_rows = min(512, length)
    blocks = length // block_rows
    scale = HEAD_DIM ** (-0.5)
    outs, logs = ([], [])
    key_index = jnp.arange(length)
    for b in range(blocks):
        seen = (b + 1) * block_rows
        q = queries[b * block_rows : seen].reshape(block_rows, heads_here, HEAD_DIM)
        k = keys[:seen].reshape(seen, heads_here, HEAD_DIM)
        v = values[:seen].reshape(seen, heads_here, HEAD_DIM)
        raw = jnp.einsum("qhd,khd->hqk", q, k, preferred_element_type=F32)
        positions = b * block_rows + jnp.arange(block_rows)
        causal = key_index[None, :seen] <= positions[:, None]
        scores = jnp.where(causal[None], raw * scale, -1e30)
        largest = jnp.max(scores, -1, keepdims=True)
        expo = jnp.exp(scores - largest)
        total = jnp.sum(expo, -1, keepdims=True)
        probs = (expo / total).astype(LOW)
        context = jnp.einsum("hqk,khd->qhd", probs, v, preferred_element_type=F32)
        outs.append(context.astype(LOW).reshape(block_rows, local_width))
        logs.append(largest + jnp.log(total))
    return (jnp.concatenate(outs, axis=0), logs)


def attention_backward(queries, keys, values, grads, logs):
    length, local_width = queries.shape
    heads_here = local_width // HEAD_DIM
    block_rows = min(512, length)
    blocks = length // block_rows
    scale = HEAD_DIM ** (-0.5)
    key_index = jnp.arange(length)
    query_grads = []
    key_sum = jnp.zeros((length, heads_here, HEAD_DIM), F32)
    value_sum = jnp.zeros((length, heads_here, HEAD_DIM), F32)
    for b in range(blocks):
        seen = (b + 1) * block_rows
        q = queries[b * block_rows : seen].reshape(block_rows, heads_here, HEAD_DIM)
        g = grads[b * block_rows : seen].reshape(block_rows, heads_here, HEAD_DIM)
        k = keys[:seen].reshape(seen, heads_here, HEAD_DIM)
        v = values[:seen].reshape(seen, heads_here, HEAD_DIM)
        raw = jnp.einsum("qhd,khd->hqk", q, k, preferred_element_type=F32)
        positions = b * block_rows + jnp.arange(block_rows)
        causal = key_index[None, :seen] <= positions[:, None]
        scores = jnp.where(causal[None], raw * scale, -1e30)
        probs = jnp.exp(scores - logs[b])
        low_probs = probs.astype(LOW)
        value_term = jnp.einsum("hqk,qhd->khd", low_probs, g, preferred_element_type=F32)
        prob_grad = jnp.einsum("qhd,khd->hqk", g, v, preferred_element_type=F32)
        score_grad = (probs * (prob_grad - jnp.sum(probs * prob_grad, -1, keepdims=True))).astype(
            LOW
        )
        query_grad = jnp.einsum("hqk,khd->qhd", score_grad, k, preferred_element_type=F32) * scale
        key_term = jnp.einsum("hqk,qhd->khd", score_grad, q, preferred_element_type=F32) * scale
        pad = ((0, length - seen), (0, 0), (0, 0))
        key_sum = key_sum + jnp.pad(key_term, pad)
        value_sum = value_sum + jnp.pad(value_term, pad)
        query_grads.append(query_grad.astype(LOW).reshape(block_rows, local_width))
    return (
        jnp.concatenate(query_grads, axis=0),
        key_sum.astype(LOW).reshape(length, local_width),
        value_sum.astype(LOW).reshape(length, local_width),
    )


def on_device(
    tokens,
    qkv_weight,
    proj_weight,
    hidden_weight,
    output_weight,
    first_gain,
    first_bias,
    second_gain,
    second_bias,
    cotangent,
):
    parts = lax.axis_size("seq")
    groups = lax.axis_size("dp")
    part = lax.axis_index("seq")
    inputs_low = tokens[0]
    rows, width = inputs_low.shape
    model_rows = qkv_weight.shape[0]
    local_width = width // parts
    hidden_rows = output_weight.shape[0] // parts
    hidden_here = hidden_rows * groups
    qkv_here = lax.dynamic_index_in_dim(
        qkv_weight.reshape(model_rows, 3, parts, local_width), part, 2, keepdims=False
    ).reshape(model_rows, 3 * local_width)
    hidden_cols = lax.dynamic_index_in_dim(
        hidden_weight.reshape(model_rows, groups, parts, hidden_rows), part, 2, keepdims=False
    ).reshape(model_rows, hidden_here)
    output_here = lax.dynamic_slice_in_dim(output_weight, part * hidden_rows, hidden_rows, 0)
    norms = jnp.stack([first_gain, first_bias, second_gain, second_bias], axis=0)
    norms = lax.all_gather(norms, "dp", axis=1, tiled=True).astype(F32)
    gain_one, bias_one, gain_two, bias_two = (norms[0], norms[1], norms[2], norms[3])
    all_tokens = gather_seq(inputs_low)
    wide_qkv = lax.all_gather(qkv_here, "dp", axis=0, tiled=True)
    wide_proj = lax.all_gather(proj_weight, "dp", axis=0, tiled=True)
    wide_hidden = lax.all_gather(hidden_cols, "dp", axis=0, tiled=True)
    wide_output = lax.all_gather(output_here, "dp", axis=0, tiled=True)
    all_grads = gather_seq(cotangent[0])
    inputs = all_tokens.astype(F32)
    lowered_one = layer_norm(inputs, gain_one, bias_one).astype(LOW)
    projected = matmul(lowered_one, wide_qkv).astype(LOW)
    queries = projected[:, :local_width]
    keys = projected[:, local_width : 2 * local_width]
    values = projected[:, 2 * local_width :]
    context_here, logs = attention_forward(queries, keys, values)
    context = lax.all_gather(context_here, "seq", axis=1, tiled=True)
    middle = inputs + matmul(context, wide_proj)
    lowered_two = layer_norm(middle, gain_two, bias_two).astype(LOW)
    hidden_pre = matmul(lowered_two, wide_hidden)
    activated_float, gelu_pull = jax.vjp(gelu_tanh, hidden_pre)
    activated = activated_float.astype(LOW)
    act_grad = matmul_right_t(all_grads, wide_output)
    pre_grad = gelu_pull(act_grad)[0].astype(LOW)
    normed_two_grad = scatter_seq(matmul_right_t(pre_grad, wide_hidden))
    ffn_out = scatter_seq(matmul(activated, wide_output))
    middle_own = lax.dynamic_slice_in_dim(middle, part * rows, rows, 0)
    block_out = middle_own + ffn_out
    _, norm_pull_two = jax.vjp(layer_norm, middle_own, gain_two, bias_two)
    middle_part, gain_two_term, bias_two_term = norm_pull_two(normed_two_grad)
    middle_grad = cotangent[0].astype(F32) + middle_part
    attn_grad = gather_seq(middle_grad.astype(LOW))
    proj_here = lax.dynamic_slice_in_dim(wide_proj, part * local_width, local_width, 0)
    context_grad = matmul_right_t(attn_grad, proj_here).astype(LOW)
    query_grads, key_grads, value_grads = attention_backward(
        queries, keys, values, context_grad, logs
    )
    qkv_grad = jnp.concatenate([query_grads, key_grads, value_grads], axis=1)
    normed_one_grad = scatter_seq(matmul_right_t(qkv_grad, wide_qkv))
    _, norm_pull_one = jax.vjp(layer_norm, inputs_low.astype(F32), gain_one, bias_one)
    input_part, gain_one_term, bias_one_term = norm_pull_one(normed_one_grad)
    tokens_gradient = (middle_grad + input_part).astype(LOW)
    attn_cols = lax.dynamic_slice_in_dim(attn_grad, part * local_width, local_width, 1)
    output_term = matmul_left_t(activated, all_grads).astype(LOW)
    hidden_term = matmul_left_t(lowered_two, pre_grad).astype(LOW)
    proj_term = matmul_left_t(context, attn_cols).astype(LOW)
    qkv_term = matmul_left_t(lowered_one, qkv_grad).astype(LOW)
    first_terms = jnp.concatenate([output_term, hidden_term], axis=1)
    second_terms = jnp.concatenate([proj_term, qkv_term], axis=1)
    first_sum = lax.psum_scatter(first_terms, "dp", scatter_dimension=0, tiled=True)
    second_sum = lax.psum_scatter(second_terms, "dp", scatter_dimension=0, tiled=True)
    first_all = lax.all_gather(first_sum, "seq", axis=0)
    second_all = lax.all_gather(second_sum, "seq", axis=0)
    output_gradient = first_all[:, :, :width].reshape(parts * hidden_rows, width).astype(F32)
    hidden_gradient = (
        first_all[:, :, width:]
        .reshape(parts, model_rows, groups, hidden_rows)
        .transpose(1, 2, 0, 3)
        .reshape(model_rows, parts * hidden_here)
        .astype(F32)
    )
    proj_gradient = (
        second_all[:, :, :local_width].transpose(1, 0, 2).reshape(model_rows, width).astype(F32)
    )
    qkv_gradient = (
        second_all[:, :, local_width:]
        .reshape(parts, model_rows, 3, local_width)
        .transpose(1, 2, 0, 3)
        .reshape(model_rows, 3 * width)
        .astype(F32)
    )
    norm_terms = jnp.stack([gain_one_term, bias_one_term, gain_two_term, bias_two_term], axis=0)
    norm_sum = lax.psum(norm_terms, ("seq", "dp"))
    norm_own = lax.dynamic_slice_in_dim(
        norm_sum, lax.axis_index("dp") * first_gain.shape[0], first_gain.shape[0], 1
    )
    return (
        block_out.astype(LOW)[None],
        tokens_gradient[None],
        qkv_gradient,
        proj_gradient,
        hidden_gradient,
        output_gradient,
        norm_own[0],
        norm_own[1],
        norm_own[2],
        norm_own[3],
    )


def solution(mesh):
    placed = (
        P("dp", "seq", None),
        P("dp", None),
        P("dp", None),
        P("dp", None),
        P("dp", None),
        P("dp"),
        P("dp"),
        P("dp"),
        P("dp"),
        P("dp", "seq", None),
    )
    return jax.shard_map(
        on_device,
        mesh=mesh,
        in_specs=placed,
        out_specs=(
            P("dp", "seq", None),
            P("dp", "seq", None),
            P("dp", None),
            P("dp", None),
            P("dp", None),
            P("dp", None),
            P("dp"),
            P("dp"),
            P("dp"),
            P("dp"),
        ),
        check_vma=False,
    )
```

profile of v0, /device:TPU:0, one launch (start us, length us, event | category | flops | bytes accessed | tf_op | source)
XLA Modules:
  0.0 499.9 jit_solution(855848961846258834)
XLA Ops:
  7.2 2.0 copy.123
  10.8 10.3 %all-gather.4 = bf16[8,96,4]{1,2,0:T(4,128)(2,1)S(1)} all-gather(bf16[1,96,4]{1,2,0:T(4,128)(2,1)S(1)} %maximum_bitcast_fusion), channel_id=1, replica_groups=mesh['seq'=4,'dp'=8] {'dp'}, dimensions={0}, use_global_device_ids=true | all-gather | bytes 6912 | tf_op jit(solution)/shard_map/all_gather | solution.py:138
  22.4 1.6 reshape.258
  24.7 11.9 %all_gather.41 = bf16[768,576]{1,0:T(8,128)(2,1)} all-gather(bf16[96,576]{1,0:T(8,128)(2,1)S(1)} %copy.126), channel_id=1, replica_groups=mesh['seq'=4,'dp'=8] {'dp'}, dimensions={0}, use_global_device_ids=true | all-gather | bytes 995328 | tf_op jit(solution)/shard_map/all_gather | solution.py:141
  36.7 13.9 %all-gather.24.cloned.1.call-done = bf16[1,1024,768]{1,2,0:T(8,128)(2,1)} async-done(((bf16[1,256,768]{1,2,0:T(8,128)(2,1)}), bf16[1,1024,768]{1,2,0:T(8,128)(2,1)}) %all-gather.24.cloned.1.call-update) | async-done | bytes 1572880 | tf_op jit(solution)/shard_map/all_gather | solution.py:35
  50.6 1.8 convert_reduce_fusion
  52.5 1.9 fusion.6
  59.2 1.5 fusion
  61.7 1.7 fusion.55
  69.1 5.8 %all-gather.16.cloned.1.call-done = bf16[768,768]{1,0:T(8,128)(2,1)} async-done(((bf16[96,768]{1,0:T(8,128)(2,1)}), bf16[768,768]{1,0:T(8,128)(2,1)}) %all-gather.16.cloned.1.call-update) | async-done | bytes 1179664 | tf_op jit(solution)/shard_map/all_gather | solution.py:142
  74.8 39.3 %all-gather.14.cloned.1.call-done = bf16[1024,768]{0,1:T(8,128)(2,1)} async-done(((bf16[1024,192]{0,1:T(8,128)(2,1)}), bf16[1024,768]{0,1:T(8,128)(2,1)}) %all-gather.14.cloned.1.call-update) | async-done | bytes 1572880 | tf_op jit(solution)/shard_map/all_gather | solution.py:153
  114.1 3.7 fusion.90
  118.5 1.7 add_convert_fusion
  120.2 19.2 %all-gather.18.cloned.1.call-done = bf16[768,768]{1,0:T(8,128)(2,1)} async-done(((bf16[96,768]{1,0:T(8,128)(2,1)}), bf16[768,768]{1,0:T(8,128)(2,1)}) %all-gather.18.cloned.1.call-update) | async-done | bytes 1179664 | tf_op jit(solution)/shard_map/all_gather | solution.py:143
  139.4 4.8 fusion.91
  144.2 21.0 %all-gather.20.cloned.1.call-done = bf16[768,768]{1,0:T(8,128)(2,1)} async-done(((bf16[96,768]{1,0:T(8,128)(2,1)}), bf16[768,768]{1,0:T(8,128)(2,1)}) %all-gather.20.cloned.1.call-update) | async-done | bytes 1179664 | tf_op jit(solution)/shard_map/all_gather | solution.py:144
  165.2 38.5 %all-gather.26.cloned.1.call-done = bf16[1,1024,768]{2,1,0:T(8,128)(2,1)} async-done(((bf16[1,256,768]{2,1,0:T(8,128)(2,1)}), bf16[1,1024,768]{2,1,0:T(8,128)(2,1)}) %all-gather.26.cloned.1.call-update) | async-done | bytes 1572880 | tf_op jit(solution)/shard_map/all_gather | solution.py:35
  203.8 5.6 %fusion.16 = bf16[1024,768]{1,0:T(8,128)(2,1)S(1)} fusion(f32[1024,768]{1,0:T(8,128)} %fusion.91, bf16[768,768]{1,0:T(8,128)(2,1)} %all-gather.20.cloned.1.call-done, bf16[1,1024,768]{2,1,0:T(8,128)(2,1)} %all-gather.26.cloned.1.call-done), kind=kOutput, calls=%fused_computation.26 | convolution fusion | flops 1223688192 | bytes 7471104 | tf_op jit(solution)/shard_map/dot_general | solution.py:31
  210.5 2.6 convolution_convert_fusion.1
  213.4 3.5 convolution_convert_fusion.3
  216.9 1.7 fusion.33
  218.6 1.5 pad_maximum_fusion
  220.2 4.3 copy.156
  224.6 1.9 copy.130
  227.2 20.3 %reduce-scatter.12.cloned.1.call-done = bf16[256,768]{0,1:T(8,128)(2,1)} async-done(((bf16[1024,768]{0,1:T(8,128)(2,1)}), bf16[256,768]{0,1:T(8,128)(2,1)}) %reduce-scatter.12.cloned.1.call-update) | async-done | bytes 393232 | tf_op jit(solution)/shard_map/reduce_scatter | solution.py:39
  247.5 2.0 multiply_reduce_fusion.3
  249.5 2.1 fusion.67
  252.2 2.7 fusion.70
  257.0 35.3 %reduce-scatter.18.cloned.1.call-done = bf16[96,1536]{1,0:T(8,128)(2,1)} async-done(((bf16[768,1536]{1,0:T(8,128)(2,1)}), bf16[96,1536]{1,0:T(8,128)(2,1)}) %reduce-scatter.18.cloned.1.call-update) | async-done | bytes 294928 | tf_op jit(solution)/shard_map/reduce_scatter | solution.py:186
  292.4 39.9 %all-gather.22.cloned.1.call-done = bf16[1024,768]{0,1:T(8,128)(2,1)} async-done(((bf16[256,768]{0,1:T(8,128)(2,1)}), bf16[1024,768]{0,1:T(8,128)(2,1)}) %all-gather.22.cloned.1.call-update) | async-done | bytes 1572880 | tf_op jit(solution)/shard_map/all_gather | solution.py:35
  332.3 2.0 convolution_convert_fusion.6
  334.4 1.5 multiply_reduce_fusion.1
  339.3 1.9 multiply_reduce_fusion
  344.0 1.7 convolution_convert_fusion.7
  351.5 2.5 convolution_convert_fusion
  354.3 5.0 %convolution_convert_fusion.2 = bf16[1024,768]{0,1:T(8,128)(2,1)} fusion(bf16[768,768]{1,0:T(8,128)(2,1)} %all-gather.20.cloned.1.call-done, f32[1024,768]{1,0:T(8,128)} %fusion.91), kind=kOutput, calls=%fused_computation.50 | convolution fusion | flops 1215823872 | bytes 5898240 | tf_op jit(solution)/shard_map/dot_general | solution.py:23
  362.5 2.4 fusion.84
  364.9 1.9 reshape.285
  366.9 2.2 copy.143
  369.0 3.6 reshape.282
  373.8 28.3 %reduce-scatter.16.cloned.1.call-done = bf16[96,768]{1,0:T(8,128)(2,1)} async-done(((bf16[768,768]{1,0:T(8,128)(2,1)}), bf16[96,768]{1,0:T(8,128)(2,1)}) %reduce-scatter.16.cloned.1.call-update) | async-done | bytes 147472 | tf_op jit(solution)/shard_map/reduce_scatter | solution.py:187
  402.0 22.2 %all-gather.2 = bf16[384,768]{1,0:T(8,128)(2,1)S(1)} all-gather(bf16[96,768]{1,0:T(8,128)(2,1)} %reduce-scatter.16.cloned.1.call-done), channel_id=4, replica_groups=mesh['seq'=4,'dp'=8] {'seq'}, dimensions={0}, use_global_device_ids=true | all-gather | bytes 737280 | tf_op jit(solution)/shard_map/all_gather | solution.py:189
  426.2 1.5 copy.140
  427.8 2.9 reshape.280
  430.7 13.6 %reduce-scatter.14.cloned.1.call-done = bf16[256,768]{0,1:T(8,128)(2,1)} async-done(((bf16[1024,768]{0,1:T(8,128)(2,1)}), bf16[256,768]{0,1:T(8,128)(2,1)}) %reduce-scatter.14.cloned.1.call-update) | async-done | bytes 393232 | tf_op jit(solution)/shard_map/reduce_scatter | solution.py:39
  445.8 1.5 fusion.68
  447.3 41.4 %psum.7 = f32[4,768]{1,0:T(4,128)S(1)} all-reduce(f32[4,768]{1,0:T(4,128)S(1)} %pad_maximum_fusion.6), channel_id=1, replica_groups=mesh['seq'=4,'dp'=8] {'seq','dp'}, use_global_device_ids=true, to_apply=%region_27.28 | all-reduce | flops 3072 | bytes 24576 | tf_op jit(solution)/shard_map/psum | solution.py:209
  489.3 2.0 fusion.73
  (212 shorter events, 42.5 us)
Async XLA Ops:
  7.2 60.5 %copy-start = (bf16[384,768]{1,0:T(8,128)(2,1)S(1)}, bf16[384,768]{1,0:T(8,128)(2,1)}, u32[]{:S(2)}) copy-start(bf16[384,768]{1,0:T(8,128)(2,1)} %param.14) | copy-start | bytes 1769476
  7.2 43.4 %all-gather.24.cloned.1.call-start = ((), (), s32[]{:S(2)}) async-start(), calls=%async_computation.13 | async-start | bytes 1966080 | tf_op jit(solution)/shard_map/all_gather | solution.py:35
  9.2 65.6 %all-gather.16.cloned.1.call-start = ((), (), s32[]{:S(2)}) async-start(), calls=%async_computation.6 | async-start | bytes 1327104 | tf_op jit(solution)/shard_map/all_gather | solution.py:142
  10.0 104.1 %all-gather.14.cloned.1.call-start = ((), (), s32[]{:S(2)}) async-start(), calls=%async_computation.5 | async-start | bytes 1966080 | tf_op jit(solution)/shard_map/all_gather | solution.py:153
  21.8 32.5 %copy-start.47 = (f32[768]{0:T(1024)}, f32[768]{0:T(1024)S(1)}, u32[]{:S(2)}) copy-start(f32[768]{0:T(1024)S(1)} %get-tuple-element.82) | copy-start | bytes 9220
  50.6 4.3 copy-start.7
  50.6 4.3 copy-start.19
  52.4 3.8 copy-start.36
  56.3 2.3 copy-start.11
  56.4 4.3 copy-start.21
  56.4 5.2 %copy-start.17 = (bf16[1024,192]{0,1:T(8,128)(2,1)}, bf16[1024,192]{0,1:T(8,128)(2,1)S(1)}, u32[]{:S(2)}) copy-start(bf16[1024,192]{0,1:T(8,128)(2,1)S(1)} %get-tuple-element.93) | copy-start | bytes 1179652
  57.2 3.5 copy-start.3
  58.7 3.0 copy-start.2
  58.7 3.0 copy-start.29
  61.7 3.0 copy-start.23
  64.2 75.2 %all-gather.18.cloned.1.call-start = ((), (), s32[]{:S(2)}) async-start(), calls=%async_computation.7 | async-start | bytes 1327104 | tf_op jit(solution)/shard_map/all_gather | solution.py:143
  67.6 97.6 %all-gather.20.cloned.1.call-start = ((), (), s32[]{:S(2)}) async-start(), calls=%async_computation.8 | async-start | bytes 1327104 | tf_op jit(solution)/shard_map/all_gather | solution.py:144
  68.4 135.3 %all-gather.26.cloned.1.call-start = ((), (), s32[]{:S(2)}) async-start(), calls=%async_computation.14 | async-start | bytes 1966080 | tf_op jit(solution)/shard_map/all_gather | solution.py:35
  69.0 178.5 %reduce-scatter.12.cloned.1.call-start = ((), (), s32[]{:S(2)}) async-start(), calls=%async_computation.10 | async-start | bytes 1966080 | tf_op jit(solution)/shard_map/reduce_scatter | solution.py:39
  117.9 131.6 %copy-start.5 = (f32[1024,768]{0,1:T(8,128)}, f32[1024,768]{0,1:T(8,128)S(1)}, u32[]{:S(2)}) copy-start(f32[1024,768]{0,1:T(8,128)S(1)} %get-tuple-element.109) | copy-start | bytes 9437188
  203.8 6.8 %copy-start.53 = (bf16[768,768]{1,0:T(8,128)(2,1)S(1)}, bf16[768,768]{1,0:T(8,128)(2,1)}, u32[]{:S(2)}) copy-start(bf16[768,768]{1,0:T(8,128)(2,1)} %all-gather.18.cloned.1.call-done) | copy-start | bytes 3538948
  213.2 79.1 %reduce-scatter.18.cloned.1.call-start = ((), (), s32[]{:S(2)}) async-start(), calls=%async_computation.17 | async-start | bytes 2654208 | tf_op jit(solution)/shard_map/reduce_scatter | solution.py:186
  213.4 3.5 copy-start.52
  213.4 3.5 copy-start.54
  224.5 107.8 %all-gather.22.cloned.1.call-start = ((), (), s32[]{:S(2)}) async-start(), calls=%async_computation.11 | async-start | bytes 1966080 | tf_op jit(solution)/shard_map/all_gather | solution.py:35
  251.6 82.8 %copy-start.4 = (f32[3,512,512]{1,2,0:T(8,128)S(1)}, f32[3,512,512]{1,2,0:T(8,128)}, u32[]{:S(2)}) copy-start(f32[3,512,512]{1,2,0:T(8,128)} %copy-done.3) | copy-start | bytes 9437188
  254.9 107.6 %all-gather.28.cloned.1.call-start = ((), (), s32[]{:S(2)}) async-start(), calls=%async_computation.15 | async-start | bytes 1474560 | tf_op jit(solution)/shard_map/all_gather | solution.py:188
  292.3 109.7 %reduce-scatter.16.cloned.1.call-start = ((), (), s32[]{:S(2)}) async-start(), calls=%async_computation.16 | async-start | bytes 1327104 | tf_op jit(solution)/shard_map/reduce_scatter | solution.py:187
  335.9 2.4 slice-start
  335.9 3.1 slice-start.1
  337.4 10.9 %copy-start.26 = (bf16[3,64,512]{2,1,0:T(8,128)(2,1)}, bf16[3,64,512]{2,1,0:T(8,128)(2,1)S(1)}, u32[]{:S(2)}) copy-start(bf16[3,64,512]{2,1,0:T(8,128)(2,1)S(1)} %fusion.52) | copy-start | bytes 589828
  342.6 3.2 copy-start.12
  344.0 4.3 copy-start.24
  351.4 92.9 %reduce-scatter.14.cloned.1.call-start = ((), (), s32[]{:S(2)}) async-start(), calls=%async_computation.12 | async-start | bytes 1966080 | tf_op jit(solution)/shard_map/reduce_scatter | solution.py:39
  354.1 5.4 %copy-start.6 = (bf16[1,256,768]{1,2,0:T(8,128)(2,1)S(1)}, bf16[1,256,768]{1,2,0:T(8,128)(2,1)}, u32[]{:S(2)}) copy-start(bf16[1,256,768]{1,2,0:T(8,128)(2,1)} %copy.123) | copy-start | bytes 1179652
  354.1 6.0 %copy-start.34 = (f32[768]{0:T(1024)S(1)}, f32[768]{0:T(1024)}, u32[]{:S(2)}) copy-start(f32[768]{0:T(1024)} %get-tuple-element.79) | copy-start | bytes 9220
  354.1 6.6 %copy-start.35 = (f32[768]{0:T(1024)S(1)}, f32[768]{0:T(1024)}, u32[]{:S(2)}) copy-start(f32[768]{0:T(1024)} %get-tuple-element.70) | copy-start | bytes 9220
  354.1 135.2 %reduce-scatter.10.cloned.1.call-start = ((), (), s32[]{:S(2)}) async-start(), calls=%async_computation.9 | async-start | bytes 1966080 | tf_op jit(solution)/shard_map/reduce_scatter | solution.py:39
  426.1 18.2 %copy-start.38 = (f32[256]{0:T(256)S(1)}, f32[256]{0:T(256)}, u32[]{:S(2)}) copy-start(f32[256]{0:T(256)} %broadcast_multiply_fusion.2) | copy-start | bytes 3076
  426.1 21.1 %copy-start.43 = (f32[1,768]{1,0:T(1,128)S(1)}, f32[1,768]{1,0:T(1,128)}, u32[]{:S(2)}) copy-start(f32[1,768]{1,0:T(1,128)} %reshape.279) | copy-start | bytes 9220
  426.1 21.1 %copy-start.44 = (f32[1,768]{1,0:T(1,128)S(1)}, f32[1,768]{1,0:T(1,128)}, u32[]{:S(2)}) copy-start(f32[1,768]{1,0:T(1,128)} %reshape.278) | copy-start | bytes 9220
  426.2 63.1 %copy-start.9 = (bf16[256,768]{0,1:T(8,128)(2,1)S(1)}, bf16[256,768]{0,1:T(8,128)(2,1)}, u32[]{:S(2)}) copy-start(bf16[256,768]{0,1:T(8,128)(2,1)} %reduce-scatter.12.cloned.1.call-done) | copy-start | bytes 1179652
  426.2 63.1 %copy-start.10 = (bf16[1,256,768]{1,2,0:T(8,128)(2,1)S(1)}, bf16[1,256,768]{1,2,0:T(8,128)(2,1)}, u32[]{:S(2)}) copy-start(bf16[1,256,768]{1,2,0:T(8,128)(2,1)} %copy.130) | copy-start | bytes 1179652
  426.2 63.1 %copy-start.32 = (f32[256]{0:T(256)S(1)}, f32[256]{0:T(256)}, u32[]{:S(2)}) copy-start(f32[256]{0:T(256)} %broadcast_multiply_fusion.3) | copy-start | bytes 3076
  426.2 63.1 %copy-start.40 = (f32[256]{0:T(256)S(1)}, f32[256]{0:T(256)}, u32[]{:S(2)}) copy-start(f32[256]{0:T(256)} %copy-done.39) | copy-start | bytes 3076
  426.2 63.1 %copy-start.42 = (f32[256]{0:T(256)S(1)}, f32[256]{0:T(256)}, u32[]{:S(2)}) copy-start(f32[256]{0:T(256)} %copy-done.41) | copy-start | bytes 3076
  426.2 63.1 %copy-start.46 = (f32[256]{0:T(256)S(1)}, f32[256]{0:T(256)}, u32[]{:S(2)}) copy-start(f32[256]{0:T(256)} %copy-done.45) | copy-start | bytes 3076
  444.3 48.9 %copy-start.1 = (bf16[384,768]{1,0:T(8,128)(2,1)S(1)}, bf16[384,768]{1,0:T(8,128)(2,1)}, u32[]{:S(2)}) copy-start(bf16[384,768]{1,0:T(8,128)(2,1)} %param.14) | copy-start | bytes 1769476
  (23 other events, 35.3 us)
Sparse Core Ops, SparseCore 0:
  10.2 40.3 all-gather.23
  52.5 22.3 all-gather.15
  77.0 37.0 all-gather.13
  116.4 22.9 all-gather.17
  141.1 24.0 all-gather.19
  166.6 37.0 all-gather.25
  213.3 34.1 reduce-scatter.11
  250.8 41.4 reduce-scatter.17
  294.5 37.6 all-gather.21
  333.8 28.7 all-gather.27
  366.1 35.8 reduce-scatter.15
  404.2 40.0 reduce-scatter.13
  446.6 35.2 reduce-scatter.9
where the time goes:
time: 508 us; the launch traced here: 500 us
  waiting for transfers between devices  278 us (55%)
  blocking collectives  85.8 us (17%)
  matrix products  48.4 us (10%)
  local copies, waits for them, and re-layouts  38.9 us (8%)
  other arithmetic  32.6 us (6%)
  between operations  15.1 us (3%)
    all_gather x3, waiting for transfers between devices, gather_seq(): return lax.all_gather(value, 'seq', axis=0, tiled=True)  92.4 us
    psum x1, blocking collectives, on_device(): norm_sum = lax.psum(norm_terms, ('seq', 'dp'))  41.4 us
    all_gather x1, waiting for transfers between devices, on_device(): context = lax.all_gather(context_here, 'seq', axis=1, tiled=True)  39.3 us
    reduce_scatter x1, waiting for transfers between devices, on_device(): lax.psum_scatter(first_terms, 'dp', scatter_dimension=0, tiled=True)  35.3 us
    reduce_scatter x3, waiting for transfers between devices, scatter_seq(): lax.psum_scatter(value.astype(LOW), 'seq', scatter_dimension=0, tiled=True)  33.9 us
    reduce_scatter x1, waiting for transfers between devices, on_device(): lax.psum_scatter(second_terms, 'dp', scatter_dimension=0, tiled=True)  28.3 us
    all_gather x1, blocking collectives, on_device(): second_all = lax.all_gather(second_sum, 'seq', axis=0)  22.2 us
    all_gather x1, waiting for transfers between devices, on_device(): wide_output = lax.all_gather(output_here, 'dp', axis=0, tiled=True)  21 us
  transfers between devices with their start and end apart: 13, of which 12 were waited for; matrix products, arithmetic and copies ran while one was open for 20% of the time, Pallas kernels for 0%

commit v1 on v0

--- a/solution.py
+++ b/solution.py
@@ -150,7 +150,18 @@
     keys = projected[:, local_width : 2 * local_width]
     values = projected[:, 2 * local_width :]
     context_here, logs = attention_forward(queries, keys, values)
-    context = lax.all_gather(context_here, "seq", axis=1, tiled=True)
+    nodes = jax.lax.axis_size("seq")
+    high = context_here
+    row_list = [high]
+    z2 = [(s - 1, s) for s in range(1, nodes)] + [(nodes - 1, 0)]
+    for _ in tuple(range(nodes - 1)):
+        high = jax.lax.ppermute(high, "seq", z2)
+        row_list += [high]
+    context = jnp.roll(
+        jnp.concatenate([*reversed(row_list)], axis=1),
+        shift=(jax.lax.axis_index("seq") + 1) * high.shape[1],
+        axis=1,
+    )
     middle = inputs + matmul(context, wide_proj)
     lowered_two = layer_norm(middle, gain_two, bias_two).astype(LOW)
     hidden_pre = matmul(lowered_two, wide_hidden)

time: 508 us -> 467 us (0.919)
  waiting for transfers between devices: 278 us -> 222 us
  local copies, waits for them, and re-layouts: 38.9 us -> 51.4 us
    all_gather x1 -> x0, waiting for transfers between devices: 39.3 us -> none  [on_device(): context = lax.all_gather(context_here, 'seq', axis=1, tiled=True)]
    ppermute x0 -> x3, waiting for transfers between devices: none -> 30.5 us  [on_device(): high = jax.lax.ppermute(high, 'seq', z2)]
    all_gather x1, waiting for transfers between devices: 19.2 us -> 0.01 us  [on_device(): wide_hidden = lax.all_gather(hidden_cols, 'dp', axis=0, tiled=True)]
    all_gather x1, waiting for transfers between devices: 21 us -> 4.46 us  [on_device(): wide_output = lax.all_gather(output_here, 'dp', axis=0, tiled=True)]
    unnamed x123 -> x147, local copies, waits for them, and re-layouts: 16.8 us -> 28.8 us
    all_gather x1, waiting for transfers between devices: 5.78 us -> 0.01 us  [on_device(): wide_proj = lax.all_gather(proj_weight, 'dp', axis=0, tiled=True)]
  transfers between devices with their start and end apart: 13 -> 15, of which waited for: 12 -> 12; matrix products, arithmetic and copies ran while one was open for 20% -> 25% of each run, Pallas kernels for 0% -> 0%
where the time goes in v1:
time: 467 us; the launch traced here: 462 us
  waiting for transfers between devices  222 us (48%)
  blocking collectives  85.2 us (18%)
  local copies, waits for them, and re-layouts  51.4 us (11%)
  matrix products  49 us (10%)
  other arithmetic  36.5 us (8%)
  between operations  15.7 us (3%)
    all_gather x3, waiting for transfers between devices, gather_seq(): return lax.all_gather(value, 'seq', axis=0, tiled=True)  87.7 us
    psum x1, blocking collectives, on_device(): norm_sum = lax.psum(norm_terms, ('seq', 'dp'))  41.2 us
    reduce_scatter x1, waiting for transfers between devices, on_device(): lax.psum_scatter(first_terms, 'dp', scatter_dimension=0, tiled=True)  35.1 us
    reduce_scatter x3, waiting for transfers between devices, scatter_seq(): lax.psum_scatter(value.astype(LOW), 'seq', scatter_dimension=0, tiled=True)  32.9 us
    ppermute x3, waiting for transfers between devices, on_device(): high = jax.lax.ppermute(high, 'seq', z2)  30.5 us
    unnamed x147, local copies, waits for them, and re-layouts  28.8 us
    reduce_scatter x1, waiting for transfers between devices, on_device(): lax.psum_scatter(second_terms, 'dp', scatter_dimension=0, tiled=True)  28.1 us
    all_gather x1, blocking collectives, on_device(): second_all = lax.all_gather(second_sum, 'seq', axis=0)  22.1 us
  transfers between devices with their start and end apart: 15, of which 12 were waited for; matrix products, arithmetic and copies ran while one was open for 25% of the time, Pallas kernels for 0%

profile of v1, /device:TPU:0, one launch (start us, length us, event | category | flops | bytes accessed | tf_op | source)
XLA Modules:
  0.0 461.7 jit_solution(7443774533642441649)
XLA Ops:
  7.3 2.0 copy.123
  10.1 2.3 reshape.268
  15.4 10.3 %all-gather.4 = bf16[8,96,4]{1,2,0:T(4,128)(2,1)S(1)} all-gather(bf16[1,96,4]{1,2,0:T(4,128)(2,1)S(1)} %maximum_bitcast_fusion), channel_id=1, replica_groups=mesh['seq'=4,'dp'=8] {'dp'}, dimensions={0}, use_global_device_ids=true | all-gather | bytes 6912 | tf_op jit(solution)/shard_map/all_gather | solution.py:138
  29.8 11.6 %all_gather.38 = bf16[768,576]{1,0:T(8,128)(2,1)S(1)} all-gather(bf16[96,576]{1,0:T(8,128)(2,1)S(1)} %copy.126), channel_id=1, replica_groups=mesh['seq'=4,'dp'=8] {'dp'}, dimensions={0}, use_global_device_ids=true | all-gather | bytes 995328 | tf_op jit(solution)/shard_map/all_gather | solution.py:141
  41.4 9.3 %all-gather.21.cloned.1.call-done = bf16[1,1024,768]{1,2,0:T(8,128)(2,1)} async-done(((bf16[1,256,768]{1,2,0:T(8,128)(2,1)}), bf16[1,1024,768]{1,2,0:T(8,128)(2,1)}) %all-gather.21.cloned.1.call-update) | async-done | bytes 1572880 | tf_op jit(solution)/shard_map/all_gather | solution.py:35
  50.7 1.8 convert_reduce_fusion
  52.5 1.9 fusion.6
  66.3 10.4 %collective-permute-done = bf16[1024,192]{0,1:T(8,128)(2,1)S(1)} collective-permute-done((bf16[1024,192]{0,1:T(8,128)(2,1)S(1)}, bf16[1024,192]{0,1:T(8,128)(2,1)S(1)}, u32[]{:S(2)}, u32[]{:S(2)}) %collective-permute-start) | collective-permute-done | bytes 393248 | tf_op jit(solution)/shard_map/ppermute | solution.py:158
  77.5 10.5 %collective-permute-done.1 = bf16[1024,192]{0,1:T(8,128)(2,1)} collective-permute-done((bf16[1024,192]{0,1:T(8,128)(2,1)S(1)}, bf16[1024,192]{0,1:T(8,128)(2,1)}, u32[]{:S(2)}, u32[]{:S(2)}) %collective-permute-start.1) | collective-permute-done | bytes 393248 | tf_op jit(solution)/shard_map/ppermute | solution.py:158
  88.3 9.6 %collective-permute-done.2 = bf16[1024,192]{0,1:T(8,128)(2,1)} collective-permute-done((bf16[1024,192]{0,1:T(8,128)(2,1)}, bf16[1024,192]{0,1:T(8,128)(2,1)}, u32[]{:S(2)}, u32[]{:S(2)}) %collective-permute-start.2) | collective-permute-done | bytes 393248 | tf_op jit(solution)/shard_map/ppermute | solution.py:158
  97.8 1.8 constant_dynamic-update-slice_fusion.7
  99.7 1.8 constant_dynamic-update-slice_fusion.6
  101.5 1.8 constant_dynamic-update-slice_fusion.5
  103.2 1.8 constant_dynamic-update-slice_fusion.4
  105.0 1.8 constant_dynamic-update-slice_fusion.3
  106.8 1.8 constant_dynamic-update-slice_fusion.2
  110.2 3.8 fusion.97
  117.4 4.8 %fusion.98 = f32[1024,768]{1,0:T(8,128)} fusion(bf16[1024,768]{0,1:T(8,128)(2,1)} %add_convert_fusion, bf16[768,768]{1,0:T(8,128)(2,1)} %all-gather.15.cloned.1.call-done), kind=kOutput, calls=%fused_computation.178 | convolution fusion | flops 1207959552 | bytes 5898240 | tf_op jit(solution)/shard_map/dot_general | solution.py:23
  122.2 4.5 all-gather.17.cloned.1.call-done
  126.7 38.5 %all-gather.23.cloned.1.call-done = bf16[1,1024,768]{2,1,0:T(8,128)(2,1)} async-done(((bf16[1,256,768]{2,1,0:T(8,128)(2,1)}), bf16[1,1024,768]{2,1,0:T(8,128)(2,1)}) %all-gather.23.cloned.1.call-update) | async-done | bytes 1572880 | tf_op jit(solution)/shard_map/all_gather | solution.py:35
  165.2 5.6 %fusion.16 = bf16[1024,768]{1,0:T(8,128)(2,1)S(1)} fusion(f32[1024,768]{1,0:T(8,128)} %fusion.98, bf16[768,768]{1,0:T(8,128)(2,1)} %all-gather.17.cloned.1.call-done, bf16[1,1024,768]{2,1,0:T(8,128)(2,1)} %all-gather.23.cloned.1.call-done), kind=kOutput, calls=%fused_computation.26 | convolution fusion | flops 1223688192 | bytes 7471104 | tf_op jit(solution)/shard_map/dot_general | solution.py:31
  172.0 2.6 convolution_convert_fusion.1
  174.7 3.5 convolution_convert_fusion.3
  178.1 1.7 fusion.33
  181.4 4.3 copy.156
  186.0 1.9 copy.130
  189.8 19.1 %reduce-scatter.12.cloned.1.call-done = bf16[256,768]{0,1:T(8,128)(2,1)} async-done(((bf16[1024,768]{0,1:T(8,128)(2,1)}), bf16[256,768]{0,1:T(8,128)(2,1)}) %reduce-scatter.12.cloned.1.call-update) | async-done | bytes 393232 | tf_op jit(solution)/shard_map/reduce_scatter | solution.py:39
  208.9 2.2 multiply_reduce_fusion.3
  211.1 2.3 fusion.73
  214.1 2.4 fusion.76
  218.6 35.1 %reduce-scatter.18.cloned.1.call-done = bf16[96,1536]{1,0:T(8,128)(2,1)} async-done(((bf16[768,1536]{1,0:T(8,128)(2,1)}), bf16[96,1536]{1,0:T(8,128)(2,1)}) %reduce-scatter.18.cloned.1.call-update) | async-done | bytes 294928 | tf_op jit(solution)/shard_map/reduce_scatter | solution.py:197
  253.8 39.9 %all-gather.19.cloned.1.call-done = bf16[1024,768]{0,1:T(8,128)(2,1)} async-done(((bf16[256,768]{0,1:T(8,128)(2,1)}), bf16[1024,768]{0,1:T(8,128)(2,1)}) %all-gather.19.cloned.1.call-update) | async-done | bytes 1572880 | tf_op jit(solution)/shard_map/all_gather | solution.py:35
  293.7 2.0 convolution_convert_fusion.6
  299.2 1.9 multiply_reduce_fusion
  304.1 2.2 fusion.51
  312.0 2.5 convolution_convert_fusion
  314.9 5.0 %convolution_convert_fusion.2 = bf16[1024,768]{0,1:T(8,128)(2,1)} fusion(bf16[768,768]{1,0:T(8,128)(2,1)} %all-gather.17.cloned.1.call-done, f32[1024,768]{1,0:T(8,128)} %fusion.98), kind=kOutput, calls=%fused_computation.50 | convolution fusion | flops 1215823872 | bytes 5898240 | tf_op jit(solution)/shard_map/dot_general | solution.py:23
  321.8 2.2 all-gather.25.cloned.1.call-done
  324.0 2.4 fusion.91
  326.4 1.9 reshape.285
  328.4 2.2 copy.143
  330.5 3.6 reshape.282
  335.3 28.1 %reduce-scatter.16.cloned.1.call-done = bf16[96,768]{1,0:T(8,128)(2,1)} async-done(((bf16[768,768]{1,0:T(8,128)(2,1)}), bf16[96,768]{1,0:T(8,128)(2,1)}) %reduce-scatter.16.cloned.1.call-update) | async-done | bytes 147472 | tf_op jit(solution)/shard_map/reduce_scatter | solution.py:198
  363.4 22.1 %all-gather.2 = bf16[384,768]{1,0:T(8,128)(2,1)S(1)} all-gather(bf16[96,768]{1,0:T(8,128)(2,1)} %reduce-scatter.16.cloned.1.call-done), channel_id=4, replica_groups=mesh['seq'=4,'dp'=8] {'seq'}, dimensions={0}, use_global_device_ids=true | all-gather | bytes 737280 | tf_op jit(solution)/shard_map/all_gather | solution.py:200
  389.0 2.9 reshape.280
  391.9 13.7 %reduce-scatter.14.cloned.1.call-done = bf16[256,768]{0,1:T(8,128)(2,1)} async-done(((bf16[1024,768]{0,1:T(8,128)(2,1)}), bf16[256,768]{0,1:T(8,128)(2,1)}) %reduce-scatter.14.cloned.1.call-update) | async-done | bytes 393232 | tf_op jit(solution)/shard_map/reduce_scatter | solution.py:39
  408.7 41.2 %psum.7 = f32[4,768]{1,0:T(4,128)S(1)} all-reduce(f32[4,768]{1,0:T(4,128)S(1)} %pad_maximum_fusion.6), channel_id=1, replica_groups=mesh['seq'=4,'dp'=8] {'seq','dp'}, use_global_device_ids=true, to_apply=%region_27.28 | all-reduce | flops 3072 | bytes 24576 | tf_op jit(solution)/shard_map/psum | solution.py:220
  450.5 2.0 fusion.79
  (241 shorter events, 57.1 us)
Async XLA Ops:
  7.2 7.4 %copy-start = (bf16[384,768]{1,0:T(8,128)(2,1)S(1)}, bf16[384,768]{1,0:T(8,128)(2,1)}, u32[]{:S(2)}) copy-start(bf16[384,768]{1,0:T(8,128)(2,1)} %param.14) | copy-start | bytes 1769476
  7.2 8.2 %copy-start.57 = (bf16[96]{0:T(256)(128)(2,1)S(1)}, bf16[96]{0:T(256)(128)(2,1)}, u32[]{:S(2)}) copy-start(bf16[96]{0:T(256)(128)(2,1)} %param.18) | copy-start | bytes 580
  7.2 8.2 %copy-start.58 = (bf16[96]{0:T(256)(128)(2,1)S(1)}, bf16[96]{0:T(256)(128)(2,1)}, u32[]{:S(2)}) copy-start(bf16[96]{0:T(256)(128)(2,1)} %param.17) | copy-start | bytes 580
  7.2 8.2 %copy-start.59 = (bf16[96]{0:T(256)(128)(2,1)S(1)}, bf16[96]{0:T(256)(128)(2,1)}, u32[]{:S(2)}) copy-start(bf16[96]{0:T(256)(128)(2,1)} %param.16) | copy-start | bytes 580
  7.2 8.2 %copy-start.60 = (bf16[96]{0:T(256)(128)(2,1)S(1)}, bf16[96]{0:T(256)(128)(2,1)}, u32[]{:S(2)}) copy-start(bf16[96]{0:T(256)(128)(2,1)} %param.15) | copy-start | bytes 580
  7.2 21.3 %copy-start.29 = (bf16[96,2304]{1,0:T(8,128)(2,1)S(1)}, bf16[96,2304]{1,0:T(8,128)(2,1)}, u32[]{:S(2)}) copy-start(bf16[96,2304]{1,0:T(8,128)(2,1)} %param.11) | copy-start | bytes 1327108
  7.2 43.4 %all-gather.21.cloned.1.call-start = ((), (), s32[]{:S(2)}) async-start(), calls=%async_computation.12 | async-start | bytes 1966080 | tf_op jit(solution)/shard_map/all_gather | solution.py:35
  9.3 100.9 %all-gather.13.cloned.1.call-start = ((), (), s32[]{:S(2)}) async-start(), calls=%async_computation.5 | async-start | bytes 1327104 | tf_op jit(solution)/shard_map/all_gather | solution.py:142
  10.1 107.3 %all-gather.15.cloned.1.call-start = ((), (), s32[]{:S(2)}) async-start(), calls=%async_computation.6 | async-start | bytes 1327104 | tf_op jit(solution)/shard_map/all_gather | solution.py:143
  14.5 112.2 %all-gather.17.cloned.1.call-start = ((), (), s32[]{:S(2)}) async-start(), calls=%async_computation.7 | async-start | bytes 1327104 | tf_op jit(solution)/shard_map/all_gather | solution.py:144
  15.3 149.9 %all-gather.23.cloned.1.call-start = ((), (), s32[]{:S(2)}) async-start(), calls=%async_computation.13 | async-start | bytes 1966080 | tf_op jit(solution)/shard_map/all_gather | solution.py:35
  26.5 27.9 %copy-start.53 = (f32[768]{0:T(1024)}, f32[768]{0:T(1024)S(1)}, u32[]{:S(2)}) copy-start(f32[768]{0:T(1024)S(1)} %get-tuple-element.82) | copy-start | bytes 9220
  41.4 14.3 %copy-start.25 = (bf16[768,576]{1,0:T(8,128)(2,1)}, bf16[768,576]{1,0:T(8,128)(2,1)S(1)}, u32[]{:S(2)}) copy-start(bf16[768,576]{1,0:T(8,128)(2,1)S(1)} %all_gather.38) | copy-start | bytes 2654212
  50.7 3.7 copy-start.5
  55.9 6.0 %copy-start.20 = (bf16[1024,192]{0,1:T(8,128)(2,1)}, bf16[1024,192]{0,1:T(8,128)(2,1)S(1)}, u32[]{:S(2)}) copy-start(bf16[1024,192]{0,1:T(8,128)(2,1)S(1)} %get-tuple-element.93) | copy-start | bytes 1179652
  58.6 6.2 %copy-start.12 = (bf16[3,64,512]{2,1,0:T(8,128)(2,1)}, bf16[3,64,512]{2,1,0:T(8,128)(2,1)S(1)}, u32[]{:S(2)}) copy-start(bf16[3,64,512]{2,1,0:T(8,128)(2,1)S(1)} %fusion.60) | copy-start | bytes 589828
  65.4 11.3 %collective-permute-start = (bf16[1024,192]{0,1:T(8,128)(2,1)S(1)}, bf16[1024,192]{0,1:T(8,128)(2,1)S(1)}, u32[]{:S(2)}, u32[]{:S(2)}) collective-permute-start(bf16[1024,192]{0,1:T(8,128)(2,1)S(1)} %pad_maximum_fusion.3), channel_id=1, source_target_pairs={{0,8},{8,16},{16,24},{24,0},{1,9},{9,17},{17,25},{25,1},{2,10},{10... | collective-permute-start | bytes 1179656 | tf_op jit(solution)/shard_map/ppermute | solution.py:158
  77.5 10.5 %collective-permute-start.1 = (bf16[1024,192]{0,1:T(8,128)(2,1)S(1)}, bf16[1024,192]{0,1:T(8,128)(2,1)}, u32[]{:S(2)}, u32[]{:S(2)}) collective-permute-start(bf16[1024,192]{0,1:T(8,128)(2,1)S(1)} %collective-permute-done), channel_id=1, source_target_pairs={{0,8},{8,16},{16,24},{24,0},{1,9},{9,17},{17,25},{25,1},{2,10},{10... | collective-permute-start | bytes 1179656 | tf_op jit(solution)/shard_map/ppermute | solution.py:158
  88.0 9.9 %collective-permute-start.2 = (bf16[1024,192]{0,1:T(8,128)(2,1)}, bf16[1024,192]{0,1:T(8,128)(2,1)}, u32[]{:S(2)}, u32[]{:S(2)}) collective-permute-start(bf16[1024,192]{0,1:T(8,128)(2,1)} %collective-permute-done.1), channel_id=1, source_target_pairs={{0,8},{8,16},{16,24},{24,0},{1,9},{9,17},{17,25},{25,1},{2,10},{10... | collective-permute-start | bytes 1179656 | tf_op jit(solution)/shard_map/ppermute | solution.py:158
  88.0 120.9 %reduce-scatter.12.cloned.1.call-start = ((), (), s32[]{:S(2)}) async-start(), calls=%async_computation.9 | async-start | bytes 1966080 | tf_op jit(solution)/shard_map/reduce_scatter | solution.py:39
  88.2 20.4 %copy-start.23 = (bf16[1024,192]{0,1:T(8,128)(2,1)S(1)}, bf16[1024,192]{0,1:T(8,128)(2,1)}, u32[]{:S(2)}) copy-start(bf16[1024,192]{0,1:T(8,128)(2,1)} %copy-done.22) | copy-start | bytes 1179652
  88.2 21.1 %copy-start.13 = (bf16[3,64,512]{2,1,0:T(8,128)(2,1)S(1)}, bf16[3,64,512]{2,1,0:T(8,128)(2,1)}, u32[]{:S(2)}) copy-start(bf16[3,64,512]{2,1,0:T(8,128)(2,1)} %copy-done.12) | copy-start | bytes 589828
  88.3 21.1 %copy-start.15 = (bf16[3,64,512]{2,1,0:T(8,128)(2,1)S(1)}, bf16[3,64,512]{2,1,0:T(8,128)(2,1)}, u32[]{:S(2)}) copy-start(bf16[3,64,512]{2,1,0:T(8,128)(2,1)} %copy-done.14) | copy-start | bytes 589828
  165.2 6.7 %copy-start.62 = (bf16[768,768]{1,0:T(8,128)(2,1)S(1)}, bf16[768,768]{1,0:T(8,128)(2,1)}, u32[]{:S(2)}) copy-start(bf16[768,768]{1,0:T(8,128)(2,1)} %all-gather.15.cloned.1.call-done) | copy-start | bytes 3538948
  174.6 79.1 %reduce-scatter.18.cloned.1.call-start = ((), (), s32[]{:S(2)}) async-start(), calls=%async_computation.16 | async-start | bytes 2654208 | tf_op jit(solution)/shard_map/reduce_scatter | solution.py:197
  174.6 3.5 copy-start.61
  174.6 3.5 copy-start.63
  185.7 107.9 %all-gather.19.cloned.1.call-start = ((), (), s32[]{:S(2)}) async-start(), calls=%async_computation.10 | async-start | bytes 1966080 | tf_op jit(solution)/shard_map/all_gather | solution.py:35
  216.5 107.5 %all-gather.25.cloned.1.call-start = ((), (), s32[]{:S(2)}) async-start(), calls=%async_computation.14 | async-start | bytes 1474560 | tf_op jit(solution)/shard_map/all_gather | solution.py:199
  253.7 109.6 %reduce-scatter.16.cloned.1.call-start = ((), (), s32[]{:S(2)}) async-start(), calls=%async_computation.15 | async-start | bytes 1327104 | tf_op jit(solution)/shard_map/reduce_scatter | solution.py:198
  302.5 3.8 copy-start.10
  303.7 5.2 %copy-start.30 = (bf16[3,64,512]{2,1,0:T(8,128)(2,1)}, bf16[3,64,512]{2,1,0:T(8,128)(2,1)S(1)}, u32[]{:S(2)}) copy-start(bf16[3,64,512]{2,1,0:T(8,128)(2,1)S(1)} %fusion.59) | copy-start | bytes 589828
  304.1 4.8 %copy-start.32 = (bf16[3,64,512]{2,1,0:T(8,128)(2,1)}, bf16[3,64,512]{2,1,0:T(8,128)(2,1)S(1)}, u32[]{:S(2)}) copy-start(bf16[3,64,512]{2,1,0:T(8,128)(2,1)S(1)} %fusion.58) | copy-start | bytes 589828
  311.9 93.8 %reduce-scatter.14.cloned.1.call-start = ((), (), s32[]{:S(2)}) async-start(), calls=%async_computation.11 | async-start | bytes 1966080 | tf_op jit(solution)/shard_map/reduce_scatter | solution.py:39
  314.5 5.4 %copy-start.4 = (bf16[1,256,768]{1,2,0:T(8,128)(2,1)S(1)}, bf16[1,256,768]{1,2,0:T(8,128)(2,1)}, u32[]{:S(2)}) copy-start(bf16[1,256,768]{1,2,0:T(8,128)(2,1)} %copy.123) | copy-start | bytes 1179652
  314.5 6.1 %copy-start.40 = (f32[768]{0:T(1024)S(1)}, f32[768]{0:T(1024)}, u32[]{:S(2)}) copy-start(f32[768]{0:T(1024)} %get-tuple-element.79) | copy-start | bytes 9220
  314.5 6.7 %copy-start.41 = (f32[768]{0:T(1024)S(1)}, f32[768]{0:T(1024)}, u32[]{:S(2)}) copy-start(f32[768]{0:T(1024)} %get-tuple-element.70) | copy-start | bytes 9220
  314.6 135.9 %reduce-scatter.10.cloned.1.call-start = ((), (), s32[]{:S(2)}) async-start(), calls=%async_computation.8 | async-start | bytes 1966080 | tf_op jit(solution)/shard_map/reduce_scatter | solution.py:39
  387.3 18.3 %copy-start.44 = (f32[256]{0:T(256)S(1)}, f32[256]{0:T(256)}, u32[]{:S(2)}) copy-start(f32[256]{0:T(256)} %broadcast_multiply_fusion.2) | copy-start | bytes 3076
  387.3 21.3 %copy-start.49 = (f32[1,768]{1,0:T(1,128)S(1)}, f32[1,768]{1,0:T(1,128)}, u32[]{:S(2)}) copy-start(f32[1,768]{1,0:T(1,128)} %reshape.279) | copy-start | bytes 9220
  387.3 21.3 %copy-start.50 = (f32[1,768]{1,0:T(1,128)S(1)}, f32[1,768]{1,0:T(1,128)}, u32[]{:S(2)}) copy-start(f32[1,768]{1,0:T(1,128)} %reshape.278) | copy-start | bytes 9220
  387.3 63.1 %copy-start.7 = (bf16[256,768]{0,1:T(8,128)(2,1)S(1)}, bf16[256,768]{0,1:T(8,128)(2,1)}, u32[]{:S(2)}) copy-start(bf16[256,768]{0,1:T(8,128)(2,1)} %reduce-scatter.12.cloned.1.call-done) | copy-start | bytes 1179652
  387.4 63.1 %copy-start.8 = (bf16[1,256,768]{1,2,0:T(8,128)(2,1)S(1)}, bf16[1,256,768]{1,2,0:T(8,128)(2,1)}, u32[]{:S(2)}) copy-start(bf16[1,256,768]{1,2,0:T(8,128)(2,1)} %copy.130) | copy-start | bytes 1179652
  387.4 63.1 %copy-start.38 = (f32[256]{0:T(256)S(1)}, f32[256]{0:T(256)}, u32[]{:S(2)}) copy-start(f32[256]{0:T(256)} %broadcast_multiply_fusion.3) | copy-start | bytes 3076
  387.4 63.1 %copy-start.46 = (f32[256]{0:T(256)S(1)}, f32[256]{0:T(256)}, u32[]{:S(2)}) copy-start(f32[256]{0:T(256)} %copy-done.45) | copy-start | bytes 3076
  387.4 63.1 %copy-start.48 = (f32[256]{0:T(256)S(1)}, f32[256]{0:T(256)}, u32[]{:S(2)}) copy-start(f32[256]{0:T(256)} %copy-done.47) | copy-start | bytes 3076
  387.4 63.1 %copy-start.52 = (f32[256]{0:T(256)S(1)}, f32[256]{0:T(256)}, u32[]{:S(2)}) copy-start(f32[256]{0:T(256)} %copy-done.51) | copy-start | bytes 3076
  405.6 48.7 %copy-start.1 = (bf16[384,768]{1,0:T(8,128)(2,1)S(1)}, bf16[384,768]{1,0:T(8,128)(2,1)}, u32[]{:S(2)}) copy-start(bf16[384,768]{1,0:T(8,128)(2,1)} %param.14) | copy-start | bytes 1769476
  (34 other events, 58.9 us)
Sparse Core Ops, SparseCore 0:
  10.2 40.3 all-gather.20
  52.5 22.2 all-gather.12
  76.8 24.0 all-gather.14
  102.6 24.0 all-gather.16
  128.1 37.0 all-gather.22
  174.7 34.1 reduce-scatter.11
  212.3 41.4 reduce-scatter.17
  255.9 37.6 all-gather.18
  295.3 28.6 all-gather.24
  327.5 35.8 reduce-scatter.15
  365.7 39.8 reduce-scatter.13
  407.8 35.1 reduce-scatter.9
